TPU v7x, 512 devices: a whole 4x4x16 slice. The times are simulated.
512 devices in a mesh: replica: 32 (over x, z_lo, core), fsdp: 16 (over y, z_hi).
Axes of the slice: x: 4, y: 4, z: 16 (z_hi: 4, z_lo: 4; z = z_hi * 4 + z_lo), core: 2. Of those that a mesh axis runs over, the one named last changes fastest.
Arguments:
- tokens: bfloat16 [131072, 5120], P(('replica', 'fsdp')), may hold values from -6 to 6
- norm_gain: float32 [5120], replicated, may hold values from 0.25 to 1.75
- key_bias: float32 [1024], replicated, may hold values from -3 to 3
- base_weights: bfloat16 [5120, 1024], P('fsdp'), may hold values from -1 to 1, as said below
- local_weights: bfloat16 [32, 5120, 1024], P('replica', 'fsdp'), may hold values from -5 to 5
- momentum: float32 [5120, 1024], P('fsdp', 'replica'), may hold values from -0.0234375 to 0.0234375
Outputs:
- key_states: bfloat16 [131072, 1024], P(('replica', 'fsdp'))
- new_momentum: float32 [5120, 1024], P('fsdp', 'replica')
Inputs may be any that keep to these rules, and one draw needn't show every extreme that they name: base_weights and local_weights are finite weights of the usual scale.
All inputs are finite; a program needn't handle non-finite values.
Results may differ from a plain program's by a relative error of at most 0.022.
Values may be sent and summed in bfloat16 or wider, within the bound.
A program may use at most 64 MiB of HBM per device.

v0:
```python
import jax
import jax.numpy as jnp
from jax import lax
from jax.sharding import PartitionSpec as P

outer_rate = 0.7
outer_beta = 0.9
epsilon = 1e-06


def per_device(tokens, norm_gain, key_bias, base_weights, local_weights, momentum):
    row_count, col_count = base_weights.shape
    groups = lax.axis_size("replica")
    owned_cols = col_count // groups
    base_wide = base_weights.astype(jnp.float32)
    quantized = lax.optimization_barrier(
        (base_wide - local_weights[0].astype(jnp.float32)).astype(jnp.bfloat16)
    )
    summed = lax.psum_scatter(
        quantized.astype(jnp.float32).astype(jnp.bfloat16),
        "replica",
        scatter_dimension=1,
        tiled=True,
    ).astype(jnp.float32)
    pseudo = summed / groups
    new_momentum = outer_beta * momentum + pseudo
    offset = lax.axis_index("replica") * owned_cols
    base_owned = lax.dynamic_slice_in_dim(base_wide, offset, owned_cols, 1)
    new_slice = (base_owned - outer_rate * (pseudo + outer_beta * new_momentum)).astype(
        jnp.bfloat16
    )
    inputs = tokens.astype(jnp.float32)
    normed = (
        inputs * lax.rsqrt(jnp.mean(inputs * inputs, axis=1, keepdims=True) + epsilon) * norm_gain
    ).astype(jnp.bfloat16)
    full_shard = lax.all_gather(new_slice, "replica", axis=1, tiled=True)
    product = jnp.dot(
        normed,
        lax.all_gather(full_shard, "fsdp", axis=0, tiled=True),
        preferred_element_type=jnp.float32,
    )
    key_states = (product + key_bias).astype(jnp.bfloat16)
    return (key_states, new_momentum)


def solution(mesh):
    return jax.shard_map(
        per_device,
        mesh=mesh,
        in_specs=(
            P(("replica", "fsdp"), None),
            P(),
            P(),
            P("fsdp", None),
            P("replica", "fsdp", None),
            P("fsdp", "replica"),
        ),
        out_specs=(P(("replica", "fsdp"), None), P("fsdp", "replica")),
        check_vma=False,
    )
```

profile of v0, /device:TPU:1, one launch (start us, length us, event | category | flops | bytes accessed | tf_op | source)
XLA Modules:
  0.0 483.1 jit_solution(12330201501924931669)
XLA Ops:
  7.2 0.0 copy-start.1
  7.2 0.0 copy-start
  7.2 0.0 reduce-scatter.4.cloned.1.call-start
  7.2 1.7 fusion.7
  8.9 0.0 copy-start.2
  8.9 0.0 copy-start.3
  8.9 1.2 copy.16
  10.1 0.0 reduce-scatter.4.cloned.1.call-update
  10.1 0.0 all-gather.2.cloned.1.call-start
  10.2 2.3 convert_element_type.31
  12.5 0.0 copy-done.1
  12.5 0.1 copy.12
  12.6 148.7 %reduce-scatter.4.cloned.1.call-done = bf16[32,320]{1,0:T(8,128)(2,1)} async-done(((bf16[1024,320]{1,0:T(8,128)(2,1)}), bf16[32,320]{1,0:T(8,128)(2,1)}) %reduce-scatter.4.cloned.1.call-update) | async-done | bytes 20496
  161.3 0.9 copy.17
  162.1 1.6 multiply_add_fusion
  163.8 0.1 copy.13
  163.9 46.0 %all_gather.6 = bf16[320,1024]{0,1:T(8,128)(2,1)S(1)} all-gather(bf16[320,32]{0,1:T(8,128)(2,1)S(1)} %copy.13), channel_id=1, replica_groups=mesh['replica'=32,'fsdp'=16] {'replica'}, dimensions={1}, use_global_device_ids=true | all-gather | bytes 675840 | tf_op jit(solution)/shard_map/all_gather | solution.py:36
  209.9 1.1 copy.14
  211.0 0.0 all-gather.2.cloned.1.call-update
  211.1 0.0 copy-done
  211.1 0.6 fusion
  211.7 1.6 copy.15
  213.3 255.2 %all-gather.2.cloned.1.call-done = bf16[5120,1024]{1,0:T(8,128)(2,1)} async-done(((bf16[320,1024]{1,0:T(8,128)(2,1)}), bf16[5120,1024]{1,0:T(8,128)(2,1)}) %all-gather.2.cloned.1.call-update) | async-done | bytes 10485776 | tf_op jit(solution)/shard_map/all_gather | solution.py:39
  468.5 0.0 copy-done.2
  468.5 0.0 copy-done.3
  468.5 7.7 %fusion.11 = bf16[256,1024]{1,0:T(8,128)(2,1)} fusion(bf16[5120,1024]{1,0:T(8,128)(2,1)} %all-gather.2.cloned.1.call-done, bf16[256,5120]{1,0:T(8,128)(2,1)S(1)} %copy-done, f32[5120]{0:T(1024)S(1)} %copy-done.2, f32[256]{0:T(256)S(1)} %add_rsqrt_fusion, f32[1024]{0:T(1024)S(1)} %copy-done.3), kind=kOutput, calls=%fused_computation.11 | convolution fusion | flops 2690121728 | bytes 13657088 | tf_op jit(solution)/shard_map/dot_general | solution.py:37
  (1 shorter events, 0.0 us)
Async XLA Ops:
  7.2 5.3 %copy-start.1 = (f32[320,32]{0,1:T(8,128)S(1)}, f32[320,32]{0,1:T(8,128)}, u32[]{:S(2)}) copy-start(f32[320,32]{0,1:T(8,128)} %param.11) | copy-start | bytes 122884
  7.2 203.9 %copy-start = (bf16[256,5120]{1,0:T(8,128)(2,1)S(1)}, bf16[256,5120]{1,0:T(8,128)(2,1)}, u32[]{:S(2)}) copy-start(bf16[256,5120]{1,0:T(8,128)(2,1)} %param.6) | copy-start | bytes 7864324
  7.2 154.1 %reduce-scatter.4.cloned.1.call-start = ((), (), s32[]{:S(2)}) async-start(), calls=%async_computation.2 | async-start | bytes 811008
  8.9 459.6 %copy-start.2 = (f32[5120]{0:T(1024)S(1)}, f32[5120]{0:T(1024)}, u32[]{:S(2)}) copy-start(f32[5120]{0:T(1024)} %param.7) | copy-start | bytes 61444
  8.9 459.6 %copy-start.3 = (f32[1024]{0:T(1024)S(1)}, f32[1024]{0:T(1024)}, u32[]{:S(2)}) copy-start(f32[1024]{0:T(1024)} %param.8) | copy-start | bytes 12292
  10.1 458.4 %all-gather.2.cloned.1.call-start = ((), (), s32[]{:S(2)}) async-start(), calls=%async_computation.1 | async-start | bytes 11141120 | tf_op jit(solution)/shard_map/all_gather | solution.py:39
Sparse Core Ops, SparseCore 0:
  10.8 150.4 reduce-scatter.3
  211.2 257.3 all-gather.1
where the time goes:
time: 483 us
  waiting for transfers between devices  404 us (84%)
  blocking collectives  46 us (10%)
  between operations  14.1 us (3%)
  matrix products  7.71 us (2%)
  other arithmetic  6.22 us (1%)
  local copies, waits for them, and re-layouts  5.02 us (1%)
    all_gather x1, waiting for transfers between devices, per_device(): lax.all_gather(full_shard, 'fsdp', axis=0, tiled=True)  255 us
    unnamed x3, waiting for transfers between devices  149 us
    all_gather x1, blocking collectives, per_device(): full_shard = lax.all_gather(new_slice, 'replica', axis=1, tiled=True)  46 us
  transfers between devices with their start and end apart: 2, of which 2 were waited for; matrix products, arithmetic and copies ran while one was open for 1% of the time, Pallas kernels for 0%

commit v1 on v0

v1 whole, which is shorter than its diff:
```python
import jax
import jax.numpy as jnp
from jax import lax
from jax.experimental import pallas as pl
from jax.experimental.pallas import tpu as pltpu
from jax.sharding import PartitionSpec as P

outer_rate = 0.7
outer_beta = 0.9
epsilon = 1e-06
MESH = pl.DeviceIdType.MESH
F32, BF16 = jnp.float32, jnp.bfloat16
REPLICAS = 32
ROWS, BLK, D, KV, TOK = 320, 80, 5120, 1024, 256
HALF = KV // 2


def kernel(
    tok_hbm, gain_hbm, bias_hbm, base_hbm, local_hbm, mom_hbm,
    out_ref, nm_ref,
    tok, gain, bias, base, local, mom,
    w, nrm, acc, send_a, recv_a, send_b, recv_b, own, send_c, recv_c,
    mom_in, mom_pad, mom_t, psum, ps_send, ps_recv, o_send, o_recv,
    in_sem, ssem, rsem, mom_ssem, mom_rsem, ps_ssem, ps_rsem,
):
    r = lax.axis_index("replica")
    f = lax.axis_index("fsdp")
    x, l, c = r // 8, (r // 2) % 4, r % 2
    y, h = f // 4, f % 4
    t = 4 * c + x
    q, qi = r // 4, r % 4
    is_self = q == t

    def rep(x_, l_, c_):
        return (x_ * 4 + l_) * 2 + c_

    def to_x(k):
        return (rep((x + k) % 4, l, c), f)

    def to_y(k):
        return (r, ((y + k) % 4) * 4 + h)

    def to_h(k):
        return (r, y * 4 + (h + k) % 4)

    def to_l(k):
        return (rep(x, (l + k) % 4, c), f)

    sib = (rep(x, l, 1 - c), f)

    loads = []
    for i, (src, dst) in enumerate(
        [(base_hbm, base), (local_hbm, local), (tok_hbm, tok), (gain_hbm, gain), (bias_hbm, bias), (mom_hbm, mom)]
    ):
        cp = pltpu.make_async_copy(src, dst, in_sem.at[i])
        cp.start()
        loads.append(cp)

    bar = pltpu.get_barrier_semaphore()

    def greet(dev):
        pl.semaphore_signal(bar, inc=1, device_id=dev, device_id_type=MESH)

    greet(sib)
    for k in (1, 2, 3):
        greet(to_x(k))
        greet(to_y(k))
        greet(to_h(k))
        greet(to_l(k))

    def mom_dest(k):
        return (rep(q % 4, k, q // 4), f)

    def mom_owner(i):
        return (4 * t + i, f)

    for k in range(4):
        @pl.when(jnp.logical_not(jnp.logical_and(is_self, l == k)))
        def _():
            greet(mom_dest(k))

        @pl.when(jnp.logical_not(jnp.logical_and(is_self, qi == k)))
        def _():
            greet(mom_owner(k))

    pl.semaphore_wait(bar, 21 - 2 * is_self.astype(jnp.int32))

    count = [0]
    pending = []

    def new_id():
        count[0] += 1
        return count[0] - 1

    def remote(i, src, dst, dev):
        return pltpu.make_async_remote_copy(src, dst, ssem.at[i], rsem.at[i], device_id=dev, device_id_type=MESH)

    def send(i, src, dst, dev):
        cp = remote(i, src, dst, dev)
        cp.start()
        pending.append(cp)

    def recv(i, dst):
        remote(i, dst, dst, sib).wait_recv()

    def tile(cc, k):
        return pl.ds(pl.multiple_of(HALF * cc + 128 * ((x + k) % 4), 128), 128)

    def quant(cols):
        return (base[:, cols].astype(F32) - local[:, cols].astype(F32)).astype(BF16)

    loads[0].wait()
    loads[1].wait()
    order = (2, 1, 3, 0)
    a_id = {k: new_id() for k in order}
    for k in order:
        send_a[k] = quant(tile(1 - c, k))
        send(a_id[k], send_a.at[k], recv_a.at[k], sib)

    loads[5].wait()
    rows_of = pl.ds(pl.multiple_of(32 * qi, 32), 32)

    def mom_remote(k):
        return pltpu.make_async_remote_copy(
            mom, mom_in.at[qi], mom_ssem.at[k], mom_rsem.at[qi], device_id=mom_dest(k), device_id_type=MESH
        )

    def mom_local():
        return pltpu.make_async_copy(mom, mom_in.at[qi], mom_rsem.at[qi])

    for k in range(4):
        mine = jnp.logical_and(is_self, l == k)

        @pl.when(jnp.logical_not(mine))
        def _():
            mom_remote(k).start()

        @pl.when(mine)
        def _():
            mom_local().start()

    b_id = {k: new_id() for k in (1, 2, 3)}
    for k in order:
        part = quant(tile(c, k)).astype(F32)
        recv(a_id[k], recv_a.at[k])
        part = part + recv_a[k].astype(F32)
        if k:
            send_b[k - 1] = part.astype(BF16)
            send(b_id[k], send_b.at[k - 1], recv_b.at[k - 1], to_x(k))
        else:
            own[...] = part

    loads[2].wait()
    loads[3].wait()
    step = 16

    def norm_rows(i, carry):
        at = pl.ds(pl.multiple_of(i * step, step), step)
        v = tok[at, :].astype(F32)
        s = lax.rsqrt(jnp.mean(v * v, axis=1, keepdims=True) + epsilon)
        o = (v * s * gain[...]).astype(BF16)
        for j in range(16):
            nrm[c, j, at, :] = o[:, ROWS * j : ROWS * (j + 1)]
        return carry

    lax.fori_loop(0, TOK // step, norm_rows, 0)
    tok_id = new_id()
    send(tok_id, nrm.at[c], nrm.at[c], sib)

    for k in (1, 3, 2):
        recv(b_id[k], recv_b.at[k - 1])
    total = own[...]
    for k in (1, 2, 3):
        total = total + recv_b[k - 1].astype(F32)
    own[...] = total
    send_c[...] = total.astype(BF16)

    def rows80(l_):
        return pl.ds(pl.multiple_of(BLK * l_, 16), BLK)

    c_id = {k: new_id() for k in (1, 2, 3)}
    for k in (1, 2, 3):
        send(c_id[k], send_c.at[rows80((l + k) % 4)], recv_c.at[k - 1], to_l(k))

    for i in range(4):
        pltpu.make_async_copy(mom, mom_in.at[i], mom_rsem.at[i]).wait()
    for i in range(4):
        mom_pad[32 * i : 32 * (i + 1), 0:ROWS] = mom_in[i]
    for j in range(3):
        mom_t[128 * j : 128 * (j + 1), :] = mom_pad[:, 128 * j : 128 * (j + 1)].T
    old = mom_t[rows80(l), :]

    for k in (1, 3, 2):
        recv(c_id[k], recv_c.at[k - 1])
    pseudo = own[rows80(l), :]
    for k in (1, 2, 3):
        pseudo = pseudo + recv_c[k - 1].astype(F32)
    pseudo = pseudo / REPLICAS
    updated = outer_beta * old + pseudo
    base_own = base[rows80(l), tile(c, 0)].astype(F32)
    w[x, y, h, l] = (base_own - outer_rate * (pseudo + outer_beta * updated)).astype(BF16)

    jump = {k: new_id() for k in (1, 2, 3)}
    quad = {(g, k): new_id() for g in range(4) for k in (1, 2, 3)}

    def block(h_, l_):
        return w.at[x, y, h_, l_]

    def send_quad(g):
        b = block((h - g) % 4, l)
        for k in (2, 1, 3):
            send(quad[g, k], b, b, to_l(k))

    for k in (2, 1, 3):
        send(jump[k], block(h, l), block(h, l), to_h(k))
    send_quad(0)

    psum[0:BLK, :] = pseudo
    ps_send[...] = psum[...].T

    def ps_remote(i):
        return pltpu.make_async_remote_copy(
            ps_send.at[32 * i : 32 * (i + 1)], ps_recv.at[l], ps_ssem.at[i], ps_rsem.at[l],
            device_id=mom_owner(i), device_id_type=MESH,
        )

    def ps_local(i):
        return pltpu.make_async_copy(ps_send.at[32 * i : 32 * (i + 1)], ps_recv.at[l], ps_rsem.at[l])

    for i in range(4):
        mine = jnp.logical_and(is_self, qi == i)

        @pl.when(jnp.logical_not(mine))
        def _():
            ps_remote(i).start()

        @pl.when(mine)
        def _():
            ps_local(i).start()

    one = {(g, d, k): new_id() for g in range(4) for d in "xy" for k in (1, 2, 3)}
    two = {(g, d, k): new_id() for g in range(4) for d in "xy" for k in (1, 2, 3)}
    lo, hi, every = pl.ds(0, 2), pl.ds(2, 2), pl.ds(0, 4)

    def one_ref(g, d, k):
        hh = (h - g) % 4
        if d == "y":
            return w.at[x, (y - k) % 4, hh, lo]
        return w.at[(x - k) % 4, y, hh, hi]

    def two_ref(g, d, k):
        hh = (h - g) % 4
        if d == "x":
            return w.at[(x - k) % 4, every, hh, lo]
        return w.at[every, (y - k) % 4, hh, hi]

    def wait_quad(g):
        for k in (1, 3, 2):
            recv(quad[g, k], block((h - g) % 4, (l - k) % 4))

    def wait_jump(g):
        recv(jump[g], block((h - g) % 4, l))

    def start_one(g):
        for k in (2, 1, 3):
            for d, to in (("y", to_y), ("x", to_x)):
                ref = one_ref(g, d, 0)
                send(one[g, d, k], ref, ref, to(k))

    def start_two(g):
        for k in (1, 3, 2):
            for d in "yx":
                recv(one[g, d, k], one_ref(g, d, k))
        for k in (2, 1, 3):
            for d, to in (("x", to_x), ("y", to_y)):
                ref = two_ref(g, d, 0)
                send(two[g, d, k], ref, ref, to(k))

    def multiply(g, first):
        for k in (1, 3, 2):
            for d in "yx":
                recv(two[g, d, k], two_ref(g, d, k))
        hh = (h - g) % 4

        def part(y_, carry):
            wt = jnp.concatenate([w[i, y_, hh].reshape(ROWS, 128) for i in range(4)], axis=1)
            for cc in range(2):
                acc[cc] += jnp.dot(nrm[cc, y_ * 4 + hh], wt, preferred_element_type=F32)
            return carry

        lax.fori_loop(0, 4, part, 0)

    acc[...] = jnp.zeros_like(acc)
    wait_quad(0)
    start_one(0)
    wait_jump(1)
    send_quad(1)
    wait_jump(3)
    send_quad(3)
    wait_jump(2)
    send_quad(2)
    start_two(0)
    wait_quad(1)
    start_one(1)
    wait_quad(3)
    start_one(3)
    wait_quad(2)
    start_one(2)

    for i in range(4):
        pltpu.make_async_copy(ps_send.at[0:32], ps_recv.at[i], ps_rsem.at[i]).wait()
    for i in range(4):
        nm_ref[:, BLK * i : BLK * (i + 1)] = (
            outer_beta * mom[:, BLK * i : BLK * (i + 1)] + ps_recv[i][:, 0:BLK]
        )

    start_two(1)
    start_two(3)
    start_two(2)
    recv(tok_id, nrm.at[1 - c])
    loads[4].wait()
    for g in (0, 1, 3, 2):
        multiply(g, g == 0)

    my_cols = pl.ds(pl.multiple_of(HALF * c, 128), HALF)
    sib_cols = pl.ds(pl.multiple_of(HALF * (1 - c), 128), HALF)
    o_send[...] = (acc[1 - c] + bias[:, my_cols]).astype(BF16)
    out_id = new_id()
    send(out_id, o_send, o_recv, sib)
    out_ref[:, my_cols] = (acc[c] + bias[:, my_cols]).astype(BF16)
    recv(out_id, o_recv)
    out_ref[:, sib_cols] = o_recv[...]

    for cp in pending:
        cp.wait_send()
    for k in range(4):
        @pl.when(jnp.logical_not(jnp.logical_and(is_self, l == k)))
        def _():
            mom_remote(k).wait_send()

        @pl.when(jnp.logical_not(jnp.logical_and(is_self, qi == k)))
        def _():
            ps_remote(k).wait_send()


TRANSFERS = 4 + 3 + 1 + 3 + 3 + 12 + 24 + 24 + 1


def per_device(tokens, norm_gain, key_bias, base_weights, local_weights, momentum):
    dma = pltpu.SemaphoreType.DMA
    key_states, new_mom = pl.pallas_call(
        kernel,
        out_shape=(
            jax.ShapeDtypeStruct((TOK, KV), BF16),
            jax.ShapeDtypeStruct((32, ROWS), F32),
        ),
        in_specs=[pl.BlockSpec(memory_space=pl.ANY)] * 6,
        out_specs=(pl.BlockSpec(memory_space=pltpu.VMEM), pl.BlockSpec(memory_space=pltpu.VMEM)),
        scratch_shapes=[
            pltpu.VMEM((TOK, D), BF16),
            pltpu.VMEM((1, D), F32),
            pltpu.VMEM((1, KV), F32),
            pltpu.VMEM((ROWS, KV), BF16),
            pltpu.VMEM((ROWS, KV), BF16),
            pltpu.VMEM((32, ROWS), F32),
            pltpu.VMEM((4, 4, 4, 4, BLK, 128), BF16),
            pltpu.VMEM((2, 16, TOK, ROWS), BF16),
            pltpu.VMEM((2, TOK, HALF), F32),
            pltpu.VMEM((4, ROWS, 128), BF16),
            pltpu.VMEM((4, ROWS, 128), BF16),
            pltpu.VMEM((3, ROWS, 128), BF16),
            pltpu.VMEM((3, ROWS, 128), BF16),
            pltpu.VMEM((ROWS, 128), F32),
            pltpu.VMEM((ROWS, 128), BF16),
            pltpu.VMEM((3, BLK, 128), BF16),
            pltpu.VMEM((4, 32, ROWS), F32),
            pltpu.VMEM((128, 384), F32),
            pltpu.VMEM((384, 128), F32),
            pltpu.VMEM((128, 128), F32),
            pltpu.VMEM((128, 128), F32),
            pltpu.VMEM((4, 32, 128), F32),
            pltpu.VMEM((TOK, HALF), BF16),
            pltpu.VMEM((TOK, HALF), BF16),
            dma((6,)),
            dma((TRANSFERS,)),
            dma((TRANSFERS,)),
            dma((4,)),
            dma((4,)),
            dma((4,)),
            dma((4,)),
        ],
        compiler_params=pltpu.CompilerParams(
            collective_id=0, has_side_effects=True, vmem_limit_bytes=56 * 1024 * 1024
        ),
        name="outer_sync",
    )(
        tokens,
        norm_gain.reshape(1, D),
        key_bias.reshape(1, KV),
        base_weights,
        local_weights.reshape(ROWS, KV),
        momentum.T,
    )
    return (key_states, new_mom.T)


def solution(mesh):
    return jax.shard_map(
        per_device,
        mesh=mesh,
        in_specs=(
            P(("replica", "fsdp"), None),
            P(),
            P(),
            P("fsdp", None),
            P("replica", "fsdp", None),
            P("fsdp", "replica"),
        ),
        out_specs=(P(("replica", "fsdp"), None), P("fsdp", "replica")),
        check_vma=False,
    )
```

time: 483 us -> 86 us (0.18)
  waiting for transfers between devices: 404 us -> 0 us
  Pallas kernels: 0 us -> 81.8 us
  blocking collectives: 46 us -> 0 us
  between operations: 14.1 us -> 0.64 us
  matrix products: 7.71 us -> 0 us
  other arithmetic: 6.22 us -> 0 us
    all_gather x1 -> x0, waiting for transfers between devices: 255 us -> none  [per_device(): lax.all_gather(full_shard, 'fsdp', axis=0, tiled=True)]
    unnamed x3 -> x0, waiting for transfers between devices: 149 us -> none
    pallas_call x0 -> x1, Pallas kernels: none -> 81.8 us  [per_device(): pl.pallas_call(kernel, out_shape=(jax.ShapeDtypeStruct((TOK, KV), BF16),...]
    all_gather x1 -> x0, blocking collectives: 46 us -> none  [per_device(): full_shard = lax.all_gather(new_slice, 'replica', axis=1, tiled=True)]
    dot_general x1 -> x0, matrix products: 7.71 us -> none  [per_device(): jnp.dot(normed, lax.all_gather(full_shard, 'fsdp', axis=0, tiled=True), p...]
  transfers between devices with their start and end apart: 2 -> 0, of which waited for: 2 -> 0; matrix products, arithmetic and copies ran while one was open for 1% -> 0% of each run, Pallas kernels for 0% -> 0%
where the time goes in v1:
time: 86 us; the launch traced here: 85.8 us
  Pallas kernels  81.8 us (95%)
  local copies, waits for them, and re-layouts  3.29 us (4%)
    pallas_call x1, Pallas kernels, per_device(): pl.pallas_call(kernel, out_shape=(jax.ShapeDtypeStruct((TOK, KV), BF16),...  81.8 us
    unnamed x2, local copies, waits for them, and re-layouts  3.29 us

profile of v1, /device:TPU:1, one launch (start us, length us, event | category | flops | bytes accessed | tf_op | source)
XLA Modules:
  0.0 85.8 jit_solution(10359746525539291256)
XLA Ops:
  0.6 81.8 %outer_sync.1 = (bf16[256,1024]{1,0:T(8,128)(2,1)}, f32[32,320]{1,0:T(8,128)}) custom-call(bf16[256,5120]{1,0:T(8,128)(2,1)} %tok_hbm.1, f32[1,5120]{1,0:T(1,128)} %bitcast.8, f32[1,1024]{1,0:T(1,128)} %bitcast.9, bf16[320,1024]{1,0:T(8,128)(2,1)} %base_hbm.1, bf16[320,1024]{1,0:T(8,128)(2,1)} %bitcast.5, f32[32,320]{1,0:T(8,128)} %bitcast.6), custom_call_target="tpu_custom_call" | custom-call | tf_op jit(solution)/shard_map/outer_sync/pallas_call | solution.py:351
  82.5 1.9 %copy.10 = bf16[256,1024]{1,0:T(8,128)(2,1)} copy(bf16[256,1024]{1,0:T(8,128)(2,1)} %get-tuple-element.8) | data formatting | bytes 1048576
  84.3 1.4 %copy.11 = f32[320,32]{0,1:T(8,128)} copy(f32[320,32]{0,1:T(8,128)} %bitcast.7) | data formatting | bytes 81920

commit v2 on v1

v2 whole, which is shorter than its diff:
```python
import jax
import jax.numpy as jnp
from jax import lax
from jax.experimental import pallas as pl
from jax.experimental.pallas import tpu as pltpu
from jax.sharding import PartitionSpec as P

outer_rate = 0.7
outer_beta = 0.9
epsilon = 1e-06
MESH = pl.DeviceIdType.MESH
F32, BF16 = jnp.float32, jnp.bfloat16
REPLICAS = 32
ROWS, BLK, D, KV, TOK = 320, 80, 5120, 1024, 256
HALF = KV // 2
A = 32


def kernel(
    tok_hbm, gain_hbm, bias_hbm, base_hbm, local_hbm, mom_hbm,
    out_hbm, nm_hbm,
    tok, gain, bias, base, local, mom, nm,
    w, nrm, acc, send_a, recv_a, own_q, send_b, recv_b, own, send_c, recv_c,
    mom_send, mom_in, mom_t, psum, ps_send, ps_recv, o_send, o_own,
    in_sem, ssem, rsem, mom_ssem, mom_rsem, ps_ssem, ps_rsem,
):
    r = lax.axis_index("replica")
    f = lax.axis_index("fsdp")
    x, l, c = r // 8, (r // 2) % 4, r % 2
    y, h = f // 4, f % 4
    z = 4 * h + l
    t = 4 * c + x
    q, qi = r // 4, r % 4
    is_self = q == t

    def rep(x_, l_, c_):
        return (x_ * 4 + l_) * 2 + c_

    def to_x(k):
        return (rep((x + k) % 4, l, c), f)

    def to_y(k):
        return (r, ((y + k) % 4) * 4 + h)

    def to_h(k):
        return (r, y * 4 + (h + k) % 4)

    def to_l(k):
        return (rep(x, (l + k) % 4, c), f)

    def to_z(k):
        z_ = (z + k) % 16
        return (rep(x, z_ % 4, c), y * 4 + z_ // 4)

    sib = (rep(x, l, 1 - c), f)

    loads = []
    for i, (src, dst) in enumerate(
        [(base_hbm, base), (local_hbm, local), (mom_hbm, mom), (tok_hbm, tok), (gain_hbm, gain), (bias_hbm, bias)]
    ):
        cp = pltpu.make_async_copy(src, dst, in_sem.at[i])
        cp.start()
        loads.append(cp)

    bar = pltpu.get_barrier_semaphore()

    def greet(dev):
        pl.semaphore_signal(bar, inc=1, device_id=dev, device_id_type=MESH)

    def mom_dest(k):
        return (rep(q % 4, k, q // 4), f)

    def mom_owner(i):
        return (4 * t + i, f)

    greet(sib)
    for k in (1, 2, 3):
        greet(to_x(k))
        greet(to_y(k))
        greet(to_h(k))
        greet(to_l(k))
    greet(to_z(1))
    greet(to_z(15))
    for k in range(4):
        @pl.when(jnp.logical_not(jnp.logical_and(is_self, l == k)))
        def _():
            greet(mom_dest(k))

        @pl.when(jnp.logical_not(jnp.logical_and(is_self, qi == k)))
        def _():
            greet(mom_owner(k))

    count = [0]
    pending = []

    def new_id(n=1):
        count[0] += n
        return count[0] - n

    def remote(i, src, dst, dev):
        return pltpu.make_async_remote_copy(src, dst, ssem.at[i], rsem.at[i], device_id=dev, device_id_type=MESH)

    def send(i, src, dst, dev):
        cp = remote(i, src, dst, dev)
        cp.start()
        pending.append(cp)

    def recv(i, dst):
        remote(i, dst, dst, sib).wait_recv()

    def tile(cc, k):
        return pl.ds(pl.multiple_of(HALF * cc + 128 * ((x + k) % 4), 128), 128)

    def quant(cols):
        return (base[:, cols].astype(F32) - local[:, cols].astype(F32)).astype(BF16)

    loads[0].wait()
    loads[1].wait()
    order = (2, 1, 3, 0)
    a_id = {k: new_id() for k in order}
    for k in order:
        send_a[k] = quant(tile(1 - c, k))
    pl.semaphore_wait(bar, 23 - 2 * is_self.astype(jnp.int32))
    for k in order:
        send(a_id[k], send_a.at[k], recv_a.at[k], sib)
    for k in order:
        own_q[k] = quant(tile(c, k))

    b_id = {k: new_id() for k in (1, 2, 3)}
    for k in order:
        recv(a_id[k], recv_a.at[k])
        part = own_q[k].astype(F32) + recv_a[k].astype(F32)
        if k:
            send_b[k - 1] = part.astype(BF16)
            send(b_id[k], send_b.at[k - 1], recv_b.at[k - 1], to_x(k))
        else:
            own[...] = part

    loads[2].wait()
    for k in range(4):
        mom_send[k, :, 0:BLK] = mom[:, BLK * k : BLK * (k + 1)]

    def mom_remote(k):
        return pltpu.make_async_remote_copy(
            mom_send.at[k], mom_in.at[qi], mom_ssem.at[k], mom_rsem.at[qi], device_id=mom_dest(k), device_id_type=MESH
        )

    def mom_local(k):
        return pltpu.make_async_copy(mom_send.at[k], mom_in.at[qi], mom_rsem.at[qi])

    for k in range(4):
        mine = jnp.logical_and(is_self, l == k)

        @pl.when(jnp.logical_not(mine))
        def _():
            mom_remote(k).start()

        @pl.when(mine)
        def _():
            mom_local(k).start()

    loads[3].wait()
    loads[4].wait()
    step = 16

    def norm_rows(i, carry):
        at = pl.ds(pl.multiple_of(i * step, step), step)
        v = tok[at, :].astype(F32)
        s = lax.rsqrt(jnp.mean(v * v, axis=1, keepdims=True) + epsilon)
        o = (v * s * gain[...]).astype(BF16)
        for j in range(16):
            nrm[c, j, at, :] = o[:, ROWS * j : ROWS * (j + 1)]
        return carry

    lax.fori_loop(0, 7, norm_rows, 0)

    for k in (1, 3, 2):
        recv(b_id[k], recv_b.at[k - 1])
    total = own[...]
    for k in (1, 2, 3):
        total = total + recv_b[k - 1].astype(F32)
    own[...] = total
    send_c[...] = total.astype(BF16)

    def rows80(l_):
        return pl.ds(pl.multiple_of(BLK * l_, 16), BLK)

    c_id = {k: new_id() for k in (1, 2, 3)}
    for k in (1, 2, 3):
        send(c_id[k], send_c.at[rows80((l + k) % 4)], recv_c.at[k - 1], to_l(k))

    for i in range(4):
        pltpu.make_async_copy(mom_send.at[0], mom_in.at[i], mom_rsem.at[i]).wait()
    mom_t[...] = mom_in[...].reshape(128, 128).T
    old = mom_t[0:BLK, :]
    lax.fori_loop(7, 10, norm_rows, 0)

    for k in (1, 3, 2):
        recv(c_id[k], recv_c.at[k - 1])
    pseudo = own[rows80(l), :]
    for k in (1, 2, 3):
        pseudo = pseudo + recv_c[k - 1].astype(F32)
    pseudo = pseudo / REPLICAS
    updated = outer_beta * old + pseudo
    base_own = base[rows80(l), tile(c, 0)].astype(F32)
    w[x, y, h, l] = (base_own - outer_rate * (pseudo + outer_beta * updated)).astype(BF16)

    groups = range(4)
    ring = (2, 1, 3)
    late = (1, 3, 2)
    jump = {k: new_id() for k in ring}
    quad = {(g, k): new_id() for g in groups for k in ring}
    ax = {(g, k): new_id() for g in groups for k in ring}
    ay = {(g, k): new_id() for g in groups for k in ring}
    az = {k: new_id(4) for k in ("up", "down", "up2", "down2")}
    one = {(g, d, k): new_id() for g in groups for d in "xy" for k in ring}
    two = {(g, d, k): new_id() for g in groups for d in "xy" for k in ("up", "down", "up2", "down2")}
    a_rows, m_rows = pl.ds(0, A), pl.ds(A, BLK - A)
    lo, hi, every = pl.ds(0, 2), pl.ds(2, 2), pl.ds(0, 4)
    x_step = {"up": 1, "down": 3}

    def grp(g):
        return (h - g) % 4

    def block(g, l_):
        return w.at[x, y, grp(g), l_, m_rows]

    def send_jumps():
        b = w.at[x, y, h, l]
        for k in ring:
            send(jump[k], b, b, to_h(k))

    def wait_jump(g):
        recv(jump[g], w.at[x, y, grp(g), l])

    def send_quad(g):
        b = block(g, l)
        for k in ring:
            send(quad[g, k], b, b, to_l(k))

    def wait_quad(g):
        for k in late:
            recv(quad[g, k], block(g, (l - k) % 4))

    def send_ax(g):
        b = w.at[x, y, grp(g), l, a_rows]
        for k in ring:
            send(ax[g, k], b, b, to_x(k))

    def ax_to_ay(g):
        for k in late:
            recv(ax[g, k], w.at[(x - k) % 4, y, grp(g), l, a_rows])
        b = w.at[every, y, grp(g), l, a_rows]
        for k in ring:
            send(ay[g, k], b, b, to_y(k))

    def az_ref(h_, l_, xs=every):
        return w.at[xs, every, h_, l_, a_rows]

    def ay_to_az(g):
        for k in late:
            recv(ay[g, k], w.at[every, (y - k) % 4, grp(g), l, a_rows])
        b = az_ref(grp(g), l)
        send(az["up"] + grp(g), b, b, to_z(1))
        send(az["down"] + grp(g), b, b, to_z(15))

    def az_on(g):
        h_ = ((z + 15) % 16 // 4 - g) % 4
        recv(az["up"] + h_, az_ref(h_, (l + 3) % 4))
        b = az_ref(h_, (l + 3) % 4, lo)
        send(az["up2"] + h_, b, b, to_z(1))
        h_ = ((z + 1) % 16 // 4 - g) % 4
        recv(az["down"] + h_, az_ref(h_, (l + 1) % 4))
        b = az_ref(h_, (l + 1) % 4, hi)
        send(az["down2"] + h_, b, b, to_z(15))

    def az_end(g):
        recv(az["up2"] + grp(g), az_ref(grp(g), (l + 2) % 4, lo))
        recv(az["down2"] + grp(g), az_ref(grp(g), (l + 2) % 4, hi))

    def one_ref(g, d, k):
        if d == "y":
            return w.at[x, (y - k) % 4, grp(g), lo, m_rows]
        return w.at[(x - k) % 4, y, grp(g), hi, m_rows]

    def two_ref(g, d, k, part=every):
        if d == "x":
            return w.at[(x - k) % 4, part, grp(g), lo, m_rows]
        return w.at[part, (y - k) % 4, grp(g), hi, m_rows]

    def send_one(g):
        for k in ring:
            for d, to in (("y", to_y), ("x", to_x)):
                b = one_ref(g, d, 0)
                send(one[g, d, k], b, b, to(k))

    def one_to_two(g):
        for d, e, to in (("y", "x", to_x), ("x", "y", to_y)):
            for k in late:
                recv(one[g, d, k], one_ref(g, d, k))
            b = two_ref(g, e, 0)
            send(two[g, e, "up"], b, b, to(1))
            send(two[g, e, "down"], b, b, to(3))

    def two_on(g):
        for e, to in (("x", to_x), ("y", to_y)):
            recv(two[g, e, "up"], two_ref(g, e, 1))
            b = two_ref(g, e, 1, lo)
            send(two[g, e, "up2"], b, b, to(1))
            recv(two[g, e, "down"], two_ref(g, e, 3))
            b = two_ref(g, e, 3, hi)
            send(two[g, e, "down2"], b, b, to(3))

    def two_end(g):
        for e in "xy":
            recv(two[g, e, "up2"], two_ref(g, e, 2, lo))
            recv(two[g, e, "down2"], two_ref(g, e, 2, hi))

    def multiply(g, cc):
        def part(y_, carry):
            wt = jnp.concatenate([w[i, y_, grp(g)].reshape(ROWS, 128) for i in range(4)], axis=1)
            acc[cc] += jnp.dot(nrm[cc, y_ * 4 + grp(g)], wt, preferred_element_type=F32)
            return carry

        lax.fori_loop(0, 4, part, 0)

    send_jumps()
    send_quad(0)
    send_ax(0)

    psum[0:BLK, :] = pseudo
    ps_send[...] = psum[...].T

    def ps_remote(i):
        return pltpu.make_async_remote_copy(
            ps_send.at[32 * i : 32 * (i + 1)], ps_recv.at[l], ps_ssem.at[i], ps_rsem.at[l],
            device_id=mom_owner(i), device_id_type=MESH,
        )

    def ps_local(i):
        return pltpu.make_async_copy(ps_send.at[32 * i : 32 * (i + 1)], ps_recv.at[l], ps_rsem.at[l])

    for i in range(4):
        mine = jnp.logical_and(is_self, qi == i)

        @pl.when(jnp.logical_not(mine))
        def _():
            ps_remote(i).start()

        @pl.when(mine)
        def _():
            ps_local(i).start()

    lax.fori_loop(10, 14, norm_rows, 0)
    ax_to_ay(0)
    wait_quad(0)
    send_one(0)
    for g in (1, 3):
        wait_jump(g)
        send_quad(g)
        send_ax(g)
    lax.fori_loop(14, 16, norm_rows, 0)
    tok_id = new_id()
    send(tok_id, nrm.at[c], nrm.at[c], sib)
    ay_to_az(0)
    wait_jump(2)
    send_quad(2)
    send_ax(2)
    one_to_two(0)
    for g in (1, 3):
        ax_to_ay(g)
    for g in (1, 3):
        wait_quad(g)
        send_one(g)
    az_on(0)
    ax_to_ay(2)
    wait_quad(2)
    send_one(2)
    for g in (1, 3):
        ay_to_az(g)
    two_on(0)
    for g in (1, 3):
        one_to_two(g)
    ay_to_az(2)
    one_to_two(2)

    for i in range(4):
        pltpu.make_async_copy(ps_send.at[0:32], ps_recv.at[i], ps_rsem.at[i]).wait()
    for i in range(4):
        nm[:, BLK * i : BLK * (i + 1)] = (
            outer_beta * mom[:, BLK * i : BLK * (i + 1)] + ps_recv[i][:, 0:BLK]
        )
    nm_out = pltpu.make_async_copy(nm, nm_hbm, in_sem.at[0])
    nm_out.start()

    acc[...] = jnp.zeros_like(acc)
    recv(tok_id, nrm.at[1 - c])
    loads[5].wait()
    for g in (1, 3):
        az_on(g)
        two_on(g)
    az_on(2)
    two_end(0)
    az_end(0)
    for cc in (0, 1):
        multiply(0, cc)
    two_on(2)
    for g in (1, 3):
        two_end(g)
        az_end(g)
        for cc in (0, 1):
            multiply(g, cc)
    two_end(2)
    az_end(2)

    my_cols = pl.ds(pl.multiple_of(HALF * c, 128), HALF)
    multiply(2, 1 - c)
    o_send[...] = (acc[1 - c] + bias[:, my_cols]).astype(BF16)
    out_id = new_id()
    send(out_id, o_send, out_hbm.at[:, my_cols], sib)
    multiply(2, c)
    o_own[...] = (acc[c] + bias[:, my_cols]).astype(BF16)
    own_out = pltpu.make_async_copy(o_own, out_hbm.at[:, my_cols], in_sem.at[1])
    own_out.start()

    for cp in pending:
        cp.wait_send()
    for k in range(4):
        @pl.when(jnp.logical_not(jnp.logical_and(is_self, l == k)))
        def _():
            mom_remote(k).wait_send()

        @pl.when(jnp.logical_not(jnp.logical_and(is_self, qi == k)))
        def _():
            ps_remote(k).wait_send()
    nm_out.wait()
    own_out.wait()
    recv(out_id, out_hbm.at[:, pl.ds(pl.multiple_of(HALF * (1 - c), 128), HALF)])
    assert count[0] == TRANSFERS


TRANSFERS = 4 + 3 + 3 + 3 + 12 + 12 + 12 + 16 + 24 + 32 + 2


def per_device(tokens, norm_gain, key_bias, base_weights, local_weights, momentum):
    dma = pltpu.SemaphoreType.DMA
    key_states, new_mom = pl.pallas_call(
        kernel,
        out_shape=(
            jax.ShapeDtypeStruct((TOK, KV), BF16),
            jax.ShapeDtypeStruct((32, ROWS), F32),
        ),
        in_specs=[pl.BlockSpec(memory_space=pl.ANY)] * 6,
        out_specs=(pl.BlockSpec(memory_space=pl.ANY), pl.BlockSpec(memory_space=pl.ANY)),
        scratch_shapes=[
            pltpu.VMEM((TOK, D), BF16),
            pltpu.VMEM((1, D), F32),
            pltpu.VMEM((1, KV), F32),
            pltpu.VMEM((ROWS, KV), BF16),
            pltpu.VMEM((ROWS, KV), BF16),
            pltpu.VMEM((32, ROWS), F32),
            pltpu.VMEM((32, ROWS), F32),
            pltpu.VMEM((4, 4, 4, 4, BLK, 128), BF16),
            pltpu.VMEM((2, 16, TOK, ROWS), BF16),
            pltpu.VMEM((2, TOK, HALF), F32),
            pltpu.VMEM((4, ROWS, 128), BF16),
            pltpu.VMEM((4, ROWS, 128), BF16),
            pltpu.VMEM((4, ROWS, 128), BF16),
            pltpu.VMEM((3, ROWS, 128), BF16),
            pltpu.VMEM((3, ROWS, 128), BF16),
            pltpu.VMEM((ROWS, 128), F32),
            pltpu.VMEM((ROWS, 128), BF16),
            pltpu.VMEM((3, BLK, 128), BF16),
            pltpu.VMEM((4, 32, 128), F32),
            pltpu.VMEM((4, 32, 128), F32),
            pltpu.VMEM((128, 128), F32),
            pltpu.VMEM((128, 128), F32),
            pltpu.VMEM((128, 128), F32),
            pltpu.VMEM((4, 32, 128), F32),
            pltpu.VMEM((TOK, HALF), BF16),
            pltpu.VMEM((TOK, HALF), BF16),
            dma((6,)),
            dma((TRANSFERS,)),
            dma((TRANSFERS,)),
            dma((4,)),
            dma((4,)),
            dma((4,)),
            dma((4,)),
        ],
        compiler_params=pltpu.CompilerParams(
            collective_id=0, has_side_effects=True, vmem_limit_bytes=56 * 1024 * 1024
        ),
        name="outer_sync",
    )(
        tokens,
        norm_gain.reshape(1, D),
        key_bias.reshape(1, KV),
        base_weights,
        local_weights.reshape(ROWS, KV),
        momentum.T,
    )
    return (key_states, new_mom.T)


def solution(mesh):
    return jax.shard_map(
        per_device,
        mesh=mesh,
        in_specs=(
            P(("replica", "fsdp"), None),
            P(),
            P(),
            P("fsdp", None),
            P("replica", "fsdp", None),
            P("fsdp", "replica"),
        ),
        out_specs=(P(("replica", "fsdp"), None), P("fsdp", "replica")),
        check_vma=False,
    )
```

time: 86 us -> 74.5 us (0.87)
  Pallas kernels: 81.8 us -> 69.8 us
    pallas_call x1, Pallas kernels: 81.8 us -> 69.8 us  [per_device(): pl.pallas_call(kernel, out_shape=(jax.ShapeDtypeStruct((TOK, KV), BF16),...]
where the time goes in v2:
time: 74.5 us; the launch traced here: 73.7 us
  Pallas kernels  69.8 us (94%)
  local copies, waits for them, and re-layouts  3.29 us (4%)
    pallas_call x1, Pallas kernels, per_device(): pl.pallas_call(kernel, out_shape=(jax.ShapeDtypeStruct((TOK, KV), BF16),...  69.8 us
    unnamed x2, local copies, waits for them, and re-layouts  3.29 us

profile of v2, /device:TPU:1, one launch (start us, length us, event | category | flops | bytes accessed | tf_op | source)
XLA Modules:
  0.0 73.7 jit_solution(12993373971402453661)
XLA Ops:
  0.6 69.8 %outer_sync.1 = (bf16[256,1024]{1,0:T(8,128)(2,1)}, f32[32,320]{1,0:T(8,128)}) custom-call(bf16[256,5120]{1,0:T(8,128)(2,1)} %tok_hbm.1, f32[1,5120]{1,0:T(1,128)} %bitcast.8, f32[1,1024]{1,0:T(1,128)} %bitcast.9, bf16[320,1024]{1,0:T(8,128)(2,1)} %base_hbm.1, bf16[320,1024]{1,0:T(8,128)(2,1)} %bitcast.5, f32[32,320]{1,0:T(8,128)} %bitcast.6), custom_call_target="tpu_custom_call" | custom-call | tf_op jit(solution)/shard_map/outer_sync/pallas_call | solution.py:447
  70.5 1.9 %copy.10 = bf16[256,1024]{1,0:T(8,128)(2,1)} copy(bf16[256,1024]{1,0:T(8,128)(2,1)} %get-tuple-element.8) | data formatting | bytes 1048576
  72.3 1.4 %copy.11 = f32[320,32]{0,1:T(8,128)} copy(f32[320,32]{0,1:T(8,128)} %bitcast.7) | data formatting | bytes 81920

commit v3 on v2

--- a/solution.py
+++ b/solution.py
@@ -18,10 +18,10 @@
 
 def kernel(
     tok_hbm, gain_hbm, bias_hbm, base_hbm, local_hbm, mom_hbm,
-    out_hbm, nm_hbm,
-    tok, gain, bias, base, local, mom, nm,
+    out_ref, nm_ref,
+    tok, gain, bias, base, local, mom,
     w, nrm, acc, send_a, recv_a, own_q, send_b, recv_b, own, send_c, recv_c,
-    mom_send, mom_in, mom_t, psum, ps_send, ps_recv, o_send, o_own,
+    mom_send, mom_in, mom_t, psum, ps_send, ps_recv, o_send,
     in_sem, ssem, rsem, mom_ssem, mom_rsem, ps_ssem, ps_rsem,
 ):
     r = lax.axis_index("replica")
@@ -169,7 +169,7 @@
         s = lax.rsqrt(jnp.mean(v * v, axis=1, keepdims=True) + epsilon)
         o = (v * s * gain[...]).astype(BF16)
         for j in range(16):
-            nrm[c, j, at, :] = o[:, ROWS * j : ROWS * (j + 1)]
+            nrm[c, j % 4, at, ROWS * (j // 4) : ROWS * (j // 4 + 1)] = o[:, ROWS * j : ROWS * (j + 1)]
         return carry
 
     lax.fori_loop(0, 7, norm_rows, 0)
@@ -203,7 +203,7 @@
     pseudo = pseudo / REPLICAS
     updated = outer_beta * old + pseudo
     base_own = base[rows80(l), tile(c, 0)].astype(F32)
-    w[x, y, h, l] = (base_own - outer_rate * (pseudo + outer_beta * updated)).astype(BF16)
+    w[x, h, y, l] = (base_own - outer_rate * (pseudo + outer_beta * updated)).astype(BF16)
 
     groups = range(4)
     ring = (2, 1, 3)
@@ -223,15 +223,15 @@
         return (h - g) % 4
 
     def block(g, l_):
-        return w.at[x, y, grp(g), l_, m_rows]
+        return w.at[x, grp(g), y, l_, m_rows]
 
     def send_jumps():
-        b = w.at[x, y, h, l]
+        b = w.at[x, h, y, l]
         for k in ring:
             send(jump[k], b, b, to_h(k))
 
     def wait_jump(g):
-        recv(jump[g], w.at[x, y, grp(g), l])
+        recv(jump[g], w.at[x, grp(g), y, l])
 
     def send_quad(g):
         b = block(g, l)
@@ -243,23 +243,23 @@
             recv(quad[g, k], block(g, (l - k) % 4))
 
     def send_ax(g):
-        b = w.at[x, y, grp(g), l, a_rows]
+        b = w.at[x, grp(g), y, l, a_rows]
         for k in ring:
             send(ax[g, k], b, b, to_x(k))
 
     def ax_to_ay(g):
         for k in late:
-            recv(ax[g, k], w.at[(x - k) % 4, y, grp(g), l, a_rows])
-        b = w.at[every, y, grp(g), l, a_rows]
+            recv(ax[g, k], w.at[(x - k) % 4, grp(g), y, l, a_rows])
+        b = w.at[every, grp(g), y, l, a_rows]
         for k in ring:
             send(ay[g, k], b, b, to_y(k))
 
     def az_ref(h_, l_, xs=every):
-        return w.at[xs, every, h_, l_, a_rows]
+        return w.at[xs, h_, every, l_, a_rows]
 
     def ay_to_az(g):
         for k in late:
-            recv(ay[g, k], w.at[every, (y - k) % 4, grp(g), l, a_rows])
+            recv(ay[g, k], w.at[every, grp(g), (y - k) % 4, l, a_rows])
         b = az_ref(grp(g), l)
         send(az["up"] + grp(g), b, b, to_z(1))
         send(az["down"] + grp(g), b, b, to_z(15))
@@ -280,13 +280,13 @@
 
     def one_ref(g, d, k):
         if d == "y":
-            return w.at[x, (y - k) % 4, grp(g), lo, m_rows]
-        return w.at[(x - k) % 4, y, grp(g), hi, m_rows]
+            return w.at[x, grp(g), (y - k) % 4, lo, m_rows]
+        return w.at[(x - k) % 4, grp(g), y, hi, m_rows]
 
     def two_ref(g, d, k, part=every):
         if d == "x":
-            return w.at[(x - k) % 4, part, grp(g), lo, m_rows]
-        return w.at[part, (y - k) % 4, grp(g), hi, m_rows]
+            return w.at[(x - k) % 4, grp(g), part, lo, m_rows]
+        return w.at[part, grp(g), (y - k) % 4, hi, m_rows]
 
     def send_one(g):
         for k in ring:
@@ -316,13 +316,12 @@
             recv(two[g, e, "up2"], two_ref(g, e, 2, lo))
             recv(two[g, e, "down2"], two_ref(g, e, 2, hi))
 
-    def multiply(g, cc):
-        def part(y_, carry):
-            wt = jnp.concatenate([w[i, y_, grp(g)].reshape(ROWS, 128) for i in range(4)], axis=1)
-            acc[cc] += jnp.dot(nrm[cc, y_ * 4 + grp(g)], wt, preferred_element_type=F32)
-            return carry
-
-        lax.fori_loop(0, 4, part, 0)
+    def multiply(g, cc, first=False):
+        for n in range(2):
+            wt = jnp.concatenate([w[2 * n + i, grp(g)].reshape(4 * ROWS, 128) for i in range(2)], axis=1)
+            part = jnp.dot(nrm[cc, grp(g)], wt, preferred_element_type=F32)
+            cols = slice(256 * n, 256 * (n + 1))
+            acc[cc, :, cols] = part if first else acc[cc, :, cols] + part
 
     send_jumps()
     send_quad(0)
@@ -387,13 +386,10 @@
     for i in range(4):
         pltpu.make_async_copy(ps_send.at[0:32], ps_recv.at[i], ps_rsem.at[i]).wait()
     for i in range(4):
-        nm[:, BLK * i : BLK * (i + 1)] = (
+        nm_ref[:, BLK * i : BLK * (i + 1)] = (
             outer_beta * mom[:, BLK * i : BLK * (i + 1)] + ps_recv[i][:, 0:BLK]
         )
-    nm_out = pltpu.make_async_copy(nm, nm_hbm, in_sem.at[0])
-    nm_out.start()
-
-    acc[...] = jnp.zeros_like(acc)
+
     recv(tok_id, nrm.at[1 - c])
     loads[5].wait()
     for g in (1, 3):
@@ -403,7 +399,7 @@
     two_end(0)
     az_end(0)
     for cc in (0, 1):
-        multiply(0, cc)
+        multiply(0, cc, True)
     two_on(2)
     for g in (1, 3):
         two_end(g)
@@ -417,11 +413,9 @@
     multiply(2, 1 - c)
     o_send[...] = (acc[1 - c] + bias[:, my_cols]).astype(BF16)
     out_id = new_id()
-    send(out_id, o_send, out_hbm.at[:, my_cols], sib)
+    send(out_id, o_send, out_ref.at[:, my_cols], sib)
     multiply(2, c)
-    o_own[...] = (acc[c] + bias[:, my_cols]).astype(BF16)
-    own_out = pltpu.make_async_copy(o_own, out_hbm.at[:, my_cols], in_sem.at[1])
-    own_out.start()
+    out_ref[:, my_cols] = (acc[c] + bias[:, my_cols]).astype(BF16)
 
     for cp in pending:
         cp.wait_send()
@@ -433,9 +427,7 @@
         @pl.when(jnp.logical_not(jnp.logical_and(is_self, qi == k)))
         def _():
             ps_remote(k).wait_send()
-    nm_out.wait()
-    own_out.wait()
-    recv(out_id, out_hbm.at[:, pl.ds(pl.multiple_of(HALF * (1 - c), 128), HALF)])
+    recv(out_id, out_ref.at[:, pl.ds(pl.multiple_of(HALF * (1 - c), 128), HALF)])
     assert count[0] == TRANSFERS
 
 
@@ -447,11 +439,11 @@
     key_states, new_mom = pl.pallas_call(
         kernel,
         out_shape=(
-            jax.ShapeDtypeStruct((TOK, KV), BF16),
-            jax.ShapeDtypeStruct((32, ROWS), F32),
+            pltpu.VMEM((TOK, KV), BF16),
+            pltpu.VMEM((32, ROWS), F32),
         ),
         in_specs=[pl.BlockSpec(memory_space=pl.ANY)] * 6,
-        out_specs=(pl.BlockSpec(memory_space=pl.ANY), pl.BlockSpec(memory_space=pl.ANY)),
+        out_specs=(pl.BlockSpec(memory_space=pltpu.VMEM), pl.BlockSpec(memory_space=pltpu.VMEM)),
         scratch_shapes=[
             pltpu.VMEM((TOK, D), BF16),
             pltpu.VMEM((1, D), F32),
@@ -459,9 +451,8 @@
             pltpu.VMEM((ROWS, KV), BF16),
             pltpu.VMEM((ROWS, KV), BF16),
             pltpu.VMEM((32, ROWS), F32),
-            pltpu.VMEM((32, ROWS), F32),
             pltpu.VMEM((4, 4, 4, 4, BLK, 128), BF16),
-            pltpu.VMEM((2, 16, TOK, ROWS), BF16),
+            pltpu.VMEM((2, 4, TOK, 4 * ROWS), BF16),
             pltpu.VMEM((2, TOK, HALF), F32),
             pltpu.VMEM((4, ROWS, 128), BF16),
             pltpu.VMEM((4, ROWS, 128), BF16),
@@ -477,7 +468,6 @@
             pltpu.VMEM((128, 128), F32),
             pltpu.VMEM((128, 128), F32),
             pltpu.VMEM((4, 32, 128), F32),
-            pltpu.VMEM((TOK, HALF), BF16),
             pltpu.VMEM((TOK, HALF), BF16),
             dma((6,)),
             dma((TRANSFERS,)),

time: 74.5 us -> 69.2 us (0.929)
  Pallas kernels: 69.8 us -> 67 us
  local copies, waits for them, and re-layouts: 3.29 us -> 1.42 us
    pallas_call x1, Pallas kernels: 69.8 us -> 67 us  [per_device(): pl.pallas_call(kernel, out_shape=(pltpu.VMEM((TOK, KV), BF16), pltpu.VMEM...]
    unnamed x2, local copies, waits for them, and re-layouts: 3.29 us -> 1.42 us
where the time goes in v3:
time: 69.2 us; the launch traced here: 69.1 us
  Pallas kernels  67 us (97%)
  local copies, waits for them, and re-layouts  1.42 us (2%)
    pallas_call x1, Pallas kernels, per_device(): pl.pallas_call(kernel, out_shape=(pltpu.VMEM((TOK, KV), BF16), pltpu.VMEM...  67 us
    unnamed x2, local copies, waits for them, and re-layouts  1.42 us

profile of v3, /device:TPU:1, one launch (start us, length us, event | category | flops | bytes accessed | tf_op | source)
XLA Modules:
  0.0 69.1 jit_solution(11961150261053363614)
XLA Ops:
  0.6 67.0 %outer_sync.1 = (bf16[256,1024]{1,0:T(8,128)(2,1)S(1)}, f32[32,320]{1,0:T(8,128)S(1)}) custom-call(bf16[256,5120]{1,0:T(8,128)(2,1)} %tok_hbm.1, f32[1,5120]{1,0:T(1,128)} %bitcast.8, f32[1,1024]{1,0:T(1,128)} %bitcast.9, bf16[320,1024]{1,0:T(8,128)(2,1)} %base_hbm.1, bf16[320,1024]{1,0:T(8,128)(2,1)} %bitcast.6, f32[32,320]{1,0:T(8,128)} %bitcast.7), custom_call_target="tpu_custom_call" | custom-call | tf_op jit(solution)/shard_map/outer_sync/pallas_call | solution.py:439
  67.7 0.8 %copy.10 = bf16[256,1024]{1,0:T(8,128)(2,1)} copy(bf16[256,1024]{1,0:T(8,128)(2,1)S(1)} %get-tuple-element.6) | data formatting | bytes 1048576
  68.5 0.6 copy.11

commit v4 on v3

--- a/solution.py
+++ b/solution.py
@@ -73,22 +73,25 @@
     def mom_owner(i):
         return (4 * t + i, f)
 
-    greet(sib)
-    for k in (1, 2, 3):
+    greet(to_h(1))
+    greet(to_h(3))
+    for k in range(4):
+        @pl.when(jnp.logical_not(jnp.logical_and(is_self, l == k)))
+        def _():
+            greet(mom_dest(k))
+
+        @pl.when(jnp.logical_not(jnp.logical_and(is_self, qi == k)))
+        def _():
+            greet(mom_owner(k))
+
+    for k in (2, 1, 3):
+        greet(to_l(k))
+    for k in (2, 1, 3):
         greet(to_x(k))
         greet(to_y(k))
-        greet(to_h(k))
-        greet(to_l(k))
     greet(to_z(1))
     greet(to_z(15))
-    for k in range(4):
-        @pl.when(jnp.logical_not(jnp.logical_and(is_self, l == k)))
-        def _():
-            greet(mom_dest(k))
-
-        @pl.when(jnp.logical_not(jnp.logical_and(is_self, qi == k)))
-        def _():
-            greet(mom_owner(k))
+    greet(sib)
 
     count = [0]
     pending = []
@@ -120,7 +123,7 @@
     a_id = {k: new_id() for k in order}
     for k in order:
         send_a[k] = quant(tile(1 - c, k))
-    pl.semaphore_wait(bar, 23 - 2 * is_self.astype(jnp.int32))
+    pl.semaphore_wait(bar, 22 - 2 * is_self.astype(jnp.int32))
     for k in order:
         send(a_id[k], send_a.at[k], recv_a.at[k], sib)
     for k in order:
@@ -209,6 +212,7 @@
     ring = (2, 1, 3)
     late = (1, 3, 2)
     jump = {k: new_id() for k in ring}
+    jump2b = new_id()
     quad = {(g, k): new_id() for g in groups for k in ring}
     ax = {(g, k): new_id() for g in groups for k in ring}
     ay = {(g, k): new_id() for g in groups for k in ring}
@@ -227,11 +231,18 @@
 
     def send_jumps():
         b = w.at[x, h, y, l]
-        for k in ring:
+        for k in (1, 3):
             send(jump[k], b, b, to_h(k))
 
     def wait_jump(g):
+        if g == 2:
+            recv(jump[2], w.at[x, grp(2), y, l, pl.ds(0, 48)])
+            recv(jump2b, w.at[x, grp(2), y, l, pl.ds(48, 32)])
+            return
         recv(jump[g], w.at[x, grp(g), y, l])
+        part = pl.ds(0, 48) if g == 1 else pl.ds(48, 32)
+        b = w.at[x, grp(g), y, l, part]
+        send(jump[2] if g == 1 else jump2b, b, b, to_h(g))
 
     def send_quad(g):
         b = block(g, l)
@@ -323,32 +334,9 @@
             cols = slice(256 * n, 256 * (n + 1))
             acc[cc, :, cols] = part if first else acc[cc, :, cols] + part
 
+    send_quad(0)
     send_jumps()
-    send_quad(0)
     send_ax(0)
-
-    psum[0:BLK, :] = pseudo
-    ps_send[...] = psum[...].T
-
-    def ps_remote(i):
-        return pltpu.make_async_remote_copy(
-            ps_send.at[32 * i : 32 * (i + 1)], ps_recv.at[l], ps_ssem.at[i], ps_rsem.at[l],
-            device_id=mom_owner(i), device_id_type=MESH,
-        )
-
-    def ps_local(i):
-        return pltpu.make_async_copy(ps_send.at[32 * i : 32 * (i + 1)], ps_recv.at[l], ps_rsem.at[l])
-
-    for i in range(4):
-        mine = jnp.logical_and(is_self, qi == i)
-
-        @pl.when(jnp.logical_not(mine))
-        def _():
-            ps_remote(i).start()
-
-        @pl.when(mine)
-        def _():
-            ps_local(i).start()
 
     lax.fori_loop(10, 14, norm_rows, 0)
     ax_to_ay(0)
@@ -383,12 +371,28 @@
     ay_to_az(2)
     one_to_two(2)
 
+    psum[0:BLK, :] = pseudo
+    ps_send[...] = psum[...].T
+
+    def ps_remote(i):
+        return pltpu.make_async_remote_copy(
+            ps_send.at[32 * i : 32 * (i + 1)], ps_recv.at[l], ps_ssem.at[i], ps_rsem.at[l],
+            device_id=mom_owner(i), device_id_type=MESH,
+        )
+
+    def ps_local(i):
+        return pltpu.make_async_copy(ps_send.at[32 * i : 32 * (i + 1)], ps_recv.at[l], ps_rsem.at[l])
+
     for i in range(4):
-        pltpu.make_async_copy(ps_send.at[0:32], ps_recv.at[i], ps_rsem.at[i]).wait()
-    for i in range(4):
-        nm_ref[:, BLK * i : BLK * (i + 1)] = (
-            outer_beta * mom[:, BLK * i : BLK * (i + 1)] + ps_recv[i][:, 0:BLK]
-        )
+        mine = jnp.logical_and(is_self, qi == i)
+
+        @pl.when(jnp.logical_not(mine))
+        def _():
+            ps_remote(i).start()
+
+        @pl.when(mine)
+        def _():
+            ps_local(i).start()
 
     recv(tok_id, nrm.at[1 - c])
     loads[5].wait()
@@ -406,6 +410,13 @@
         az_end(g)
         for cc in (0, 1):
             multiply(g, cc)
+    for i in range(4):
+        pltpu.make_async_copy(ps_send.at[0:32], ps_recv.at[i], ps_rsem.at[i]).wait()
+    for i in range(4):
+        nm_ref[:, BLK * i : BLK * (i + 1)] = (
+            outer_beta * mom[:, BLK * i : BLK * (i + 1)] + ps_recv[i][:, 0:BLK]
+        )
+
     two_end(2)
     az_end(2)
 
@@ -431,7 +442,7 @@
     assert count[0] == TRANSFERS
 
 
-TRANSFERS = 4 + 3 + 3 + 3 + 12 + 12 + 12 + 16 + 24 + 32 + 2
+TRANSFERS = 5 + 3 + 3 + 3 + 12 + 12 + 12 + 16 + 24 + 32 + 2
 
 
 def per_device(tokens, norm_gain, key_bias, base_weights, local_weights, momentum):

time: 69.2 us -> 67.3 us (0.973)
  Pallas kernels: 67 us -> 65.1 us
    pallas_call x1, Pallas kernels: 67 us -> 65.1 us  [per_device(): pl.pallas_call(kernel, out_shape=(pltpu.VMEM((TOK, KV), BF16), pltpu.VMEM...]
where the time goes in v4:
time: 67.3 us; the launch traced here: 67.2 us
  Pallas kernels  65.1 us (97%)
  local copies, waits for them, and re-layouts  1.42 us (2%)
    pallas_call x1, Pallas kernels, per_device(): pl.pallas_call(kernel, out_shape=(pltpu.VMEM((TOK, KV), BF16), pltpu.VMEM...  65.1 us
    unnamed x2, local copies, waits for them, and re-layouts  1.42 us

profile of v4, /device:TPU:1, one launch (start us, length us, event | category | flops | bytes accessed | tf_op | source)
XLA Modules:
  0.0 67.2 jit_solution(10823408479465006346)
XLA Ops:
  0.6 65.1 %outer_sync.1 = (bf16[256,1024]{1,0:T(8,128)(2,1)S(1)}, f32[32,320]{1,0:T(8,128)S(1)}) custom-call(bf16[256,5120]{1,0:T(8,128)(2,1)} %tok_hbm.1, f32[1,5120]{1,0:T(1,128)} %bitcast.8, f32[1,1024]{1,0:T(1,128)} %bitcast.9, bf16[320,1024]{1,0:T(8,128)(2,1)} %base_hbm.1, bf16[320,1024]{1,0:T(8,128)(2,1)} %bitcast.6, f32[32,320]{1,0:T(8,128)} %bitcast.7), custom_call_target="tpu_custom_call" | custom-call | tf_op jit(solution)/shard_map/outer_sync/pallas_call | solution.py:450
  65.8 0.8 %copy.10 = bf16[256,1024]{1,0:T(8,128)(2,1)} copy(bf16[256,1024]{1,0:T(8,128)(2,1)S(1)} %get-tuple-element.6) | data formatting | bytes 1048576
  66.6 0.6 copy.11

commit v5 on v4

--- a/solution.py
+++ b/solution.py
@@ -91,6 +91,8 @@
         greet(to_y(k))
     greet(to_z(1))
     greet(to_z(15))
+    greet(to_z(2))
+    greet(to_z(14))
     greet(sib)
 
     count = [0]
@@ -123,7 +125,7 @@
     a_id = {k: new_id() for k in order}
     for k in order:
         send_a[k] = quant(tile(1 - c, k))
-    pl.semaphore_wait(bar, 22 - 2 * is_self.astype(jnp.int32))
+    pl.semaphore_wait(bar, 24 - 2 * is_self.astype(jnp.int32))
     for k in order:
         send(a_id[k], send_a.at[k], recv_a.at[k], sib)
     for k in order:
@@ -274,16 +276,23 @@
         b = az_ref(grp(g), l)
         send(az["up"] + grp(g), b, b, to_z(1))
         send(az["down"] + grp(g), b, b, to_z(15))
+        if g == 2:
+            b = az_ref(grp(g), l, lo)
+            send(az["up2"] + grp(g), b, b, to_z(2))
+            b = az_ref(grp(g), l, hi)
+            send(az["down2"] + grp(g), b, b, to_z(14))
 
     def az_on(g):
         h_ = ((z + 15) % 16 // 4 - g) % 4
         recv(az["up"] + h_, az_ref(h_, (l + 3) % 4))
         b = az_ref(h_, (l + 3) % 4, lo)
-        send(az["up2"] + h_, b, b, to_z(1))
+        if g != 2:
+            send(az["up2"] + h_, b, b, to_z(1))
         h_ = ((z + 1) % 16 // 4 - g) % 4
         recv(az["down"] + h_, az_ref(h_, (l + 1) % 4))
         b = az_ref(h_, (l + 1) % 4, hi)
-        send(az["down2"] + h_, b, b, to_z(15))
+        if g != 2:
+            send(az["down2"] + h_, b, b, to_z(15))
 
     def az_end(g):
         recv(az["up2"] + grp(g), az_ref(grp(g), (l + 2) % 4, lo))
@@ -312,15 +321,21 @@
             b = two_ref(g, e, 0)
             send(two[g, e, "up"], b, b, to(1))
             send(two[g, e, "down"], b, b, to(3))
+            if g == 2:
+                for key, half in (("up2", lo), ("down2", hi)):
+                    b = two_ref(g, e, 0, half)
+                    send(two[g, e, key], b, b, to(2))
 
     def two_on(g):
         for e, to in (("x", to_x), ("y", to_y)):
             recv(two[g, e, "up"], two_ref(g, e, 1))
             b = two_ref(g, e, 1, lo)
-            send(two[g, e, "up2"], b, b, to(1))
+            if g != 2:
+                send(two[g, e, "up2"], b, b, to(1))
             recv(two[g, e, "down"], two_ref(g, e, 3))
             b = two_ref(g, e, 3, hi)
-            send(two[g, e, "down2"], b, b, to(3))
+            if g != 2:
+                send(two[g, e, "down2"], b, b, to(3))
 
     def two_end(g):
         for e in "xy":
@@ -350,25 +365,29 @@
     tok_id = new_id()
     send(tok_id, nrm.at[c], nrm.at[c], sib)
     ay_to_az(0)
+    one_to_two(0)
+    for g in (1, 3):
+        ax_to_ay(g)
+    for g in (1, 3):
+        wait_quad(g)
+        send_one(g)
+    az_on(0)
     wait_jump(2)
     send_quad(2)
     send_ax(2)
-    one_to_two(0)
-    for g in (1, 3):
-        ax_to_ay(g)
-    for g in (1, 3):
-        wait_quad(g)
-        send_one(g)
-    az_on(0)
-    ax_to_ay(2)
+    two_on(0)
+    for g in (1, 3):
+        ay_to_az(g)
+    for g in (1, 3):
+        one_to_two(g)
     wait_quad(2)
     send_one(2)
-    for g in (1, 3):
-        ay_to_az(g)
-    two_on(0)
-    for g in (1, 3):
-        one_to_two(g)
+    ax_to_ay(2)
+    for g in (1, 3):
+        az_on(g)
     ay_to_az(2)
+    for g in (1, 3):
+        two_on(g)
     one_to_two(2)
 
     psum[0:BLK, :] = pseudo
@@ -396,15 +415,12 @@
 
     recv(tok_id, nrm.at[1 - c])
     loads[5].wait()
-    for g in (1, 3):
-        az_on(g)
-        two_on(g)
     az_on(2)
+    two_on(2)
     two_end(0)
     az_end(0)
     for cc in (0, 1):
         multiply(0, cc, True)
-    two_on(2)
     for g in (1, 3):
         two_end(g)
         az_end(g)

time: 67.3 us -> 65.2 us (0.969)
  Pallas kernels: 65.1 us -> 63 us
    pallas_call x1, Pallas kernels: 65.1 us -> 63 us  [per_device(): pl.pallas_call(kernel, out_shape=(pltpu.VMEM((TOK, KV), BF16), pltpu.VMEM...]
where the time goes in v5:
time: 65.2 us; the launch traced here: 65.1 us
  Pallas kernels  63 us (97%)
  local copies, waits for them, and re-layouts  1.42 us (2%)
    pallas_call x1, Pallas kernels, per_device(): pl.pallas_call(kernel, out_shape=(pltpu.VMEM((TOK, KV), BF16), pltpu.VMEM...  63 us
    unnamed x2, local copies, waits for them, and re-layouts  1.42 us

profile of v5, /device:TPU:1, one launch (start us, length us, event | category | flops | bytes accessed | tf_op | source)
XLA Modules:
  0.0 65.1 jit_solution(3100944047089134172)
XLA Ops:
  0.6 63.0 %outer_sync.1 = (bf16[256,1024]{1,0:T(8,128)(2,1)S(1)}, f32[32,320]{1,0:T(8,128)S(1)}) custom-call(bf16[256,5120]{1,0:T(8,128)(2,1)} %tok_hbm.1, f32[1,5120]{1,0:T(1,128)} %bitcast.8, f32[1,1024]{1,0:T(1,128)} %bitcast.9, bf16[320,1024]{1,0:T(8,128)(2,1)} %base_hbm.1, bf16[320,1024]{1,0:T(8,128)(2,1)} %bitcast.6, f32[32,320]{1,0:T(8,128)} %bitcast.7), custom_call_target="tpu_custom_call" | custom-call | tf_op jit(solution)/shard_map/outer_sync/pallas_call | solution.py:466
  63.7 0.8 %copy.10 = bf16[256,1024]{1,0:T(8,128)(2,1)} copy(bf16[256,1024]{1,0:T(8,128)(2,1)S(1)} %get-tuple-element.6) | data formatting | bytes 1048576
  64.5 0.6 copy.11

commit v6 on v5

--- a/solution.py
+++ b/solution.py
@@ -143,7 +143,7 @@
 
     loads[2].wait()
     for k in range(4):
-        mom_send[k, :, 0:BLK] = mom[:, BLK * k : BLK * (k + 1)]
+        mom_send[k, :, 0:BLK] = mom[:, BLK * k : BLK * (k + 1)].astype(BF16)
 
     def mom_remote(k):
         return pltpu.make_async_remote_copy(
@@ -196,7 +196,7 @@
 
     for i in range(4):
         pltpu.make_async_copy(mom_send.at[0], mom_in.at[i], mom_rsem.at[i]).wait()
-    mom_t[...] = mom_in[...].reshape(128, 128).T
+    mom_t[...] = mom_in[...].astype(F32).reshape(128, 128).T
     old = mom_t[0:BLK, :]
     lax.fori_loop(7, 10, norm_rows, 0)
 
@@ -391,7 +391,7 @@
     one_to_two(2)
 
     psum[0:BLK, :] = pseudo
-    ps_send[...] = psum[...].T
+    ps_send[...] = psum[...].T.astype(BF16)
 
     def ps_remote(i):
         return pltpu.make_async_remote_copy(
@@ -430,7 +430,7 @@
         pltpu.make_async_copy(ps_send.at[0:32], ps_recv.at[i], ps_rsem.at[i]).wait()
     for i in range(4):
         nm_ref[:, BLK * i : BLK * (i + 1)] = (
-            outer_beta * mom[:, BLK * i : BLK * (i + 1)] + ps_recv[i][:, 0:BLK]
+            outer_beta * mom[:, BLK * i : BLK * (i + 1)] + ps_recv[i][:, 0:BLK].astype(F32)
         )
 
     two_end(2)
@@ -489,12 +489,12 @@
             pltpu.VMEM((ROWS, 128), F32),
             pltpu.VMEM((ROWS, 128), BF16),
             pltpu.VMEM((3, BLK, 128), BF16),
-            pltpu.VMEM((4, 32, 128), F32),
-            pltpu.VMEM((4, 32, 128), F32),
+            pltpu.VMEM((4, 32, 128), BF16),
+            pltpu.VMEM((4, 32, 128), BF16),
             pltpu.VMEM((128, 128), F32),
             pltpu.VMEM((128, 128), F32),
-            pltpu.VMEM((128, 128), F32),
-            pltpu.VMEM((4, 32, 128), F32),
+            pltpu.VMEM((128, 128), BF16),
+            pltpu.VMEM((4, 32, 128), BF16),
             pltpu.VMEM((TOK, HALF), BF16),
             dma((6,)),
             dma((TRANSFERS,)),

time: 65.2 us -> 64.9 us (level)
  no operation moved by 1% of the time
where the time goes in v6:
time: 64.9 us; the launch traced here: 64.8 us
  Pallas kernels  62.7 us (97%)
  local copies, waits for them, and re-layouts  1.42 us (2%)
    pallas_call x1, Pallas kernels, per_device(): pl.pallas_call(kernel, out_shape=(pltpu.VMEM((TOK, KV), BF16), pltpu.VMEM...  62.7 us
    unnamed x2, local copies, waits for them, and re-layouts  1.42 us

profile of v6, /device:TPU:1, one launch (start us, length us, event | category | flops | bytes accessed | tf_op | source)
XLA Modules:
  0.0 64.8 jit_solution(6283445607430706703)
XLA Ops:
  0.6 62.7 %outer_sync.1 = (bf16[256,1024]{1,0:T(8,128)(2,1)S(1)}, f32[32,320]{1,0:T(8,128)S(1)}) custom-call(bf16[256,5120]{1,0:T(8,128)(2,1)} %tok_hbm.1, f32[1,5120]{1,0:T(1,128)} %bitcast.8, f32[1,1024]{1,0:T(1,128)} %bitcast.9, bf16[320,1024]{1,0:T(8,128)(2,1)} %base_hbm.1, bf16[320,1024]{1,0:T(8,128)(2,1)} %bitcast.6, f32[32,320]{1,0:T(8,128)} %bitcast.7), custom_call_target="tpu_custom_call" | custom-call | tf_op jit(solution)/shard_map/outer_sync/pallas_call | solution.py:466
  63.4 0.8 %copy.10 = bf16[256,1024]{1,0:T(8,128)(2,1)} copy(bf16[256,1024]{1,0:T(8,128)(2,1)S(1)} %get-tuple-element.6) | data formatting | bytes 1048576
  64.2 0.6 copy.11

commit v7 on v6

--- a/solution.py
+++ b/solution.py
@@ -141,29 +141,6 @@
         else:
             own[...] = part
 
-    loads[2].wait()
-    for k in range(4):
-        mom_send[k, :, 0:BLK] = mom[:, BLK * k : BLK * (k + 1)].astype(BF16)
-
-    def mom_remote(k):
-        return pltpu.make_async_remote_copy(
-            mom_send.at[k], mom_in.at[qi], mom_ssem.at[k], mom_rsem.at[qi], device_id=mom_dest(k), device_id_type=MESH
-        )
-
-    def mom_local(k):
-        return pltpu.make_async_copy(mom_send.at[k], mom_in.at[qi], mom_rsem.at[qi])
-
-    for k in range(4):
-        mine = jnp.logical_and(is_self, l == k)
-
-        @pl.when(jnp.logical_not(mine))
-        def _():
-            mom_remote(k).start()
-
-        @pl.when(mine)
-        def _():
-            mom_local(k).start()
-
     loads[3].wait()
     loads[4].wait()
     step = 16
@@ -178,6 +155,29 @@
         return carry
 
     lax.fori_loop(0, 7, norm_rows, 0)
+
+    loads[2].wait()
+    for k in range(4):
+        mom_send[k, :, 0:BLK] = mom[:, BLK * k : BLK * (k + 1)].astype(BF16)
+
+    def mom_remote(k):
+        return pltpu.make_async_remote_copy(
+            mom_send.at[k], mom_in.at[qi], mom_ssem.at[k], mom_rsem.at[qi], device_id=mom_dest(k), device_id_type=MESH
+        )
+
+    def mom_local(k):
+        return pltpu.make_async_copy(mom_send.at[k], mom_in.at[qi], mom_rsem.at[qi])
+
+    for k in range(4):
+        mine = jnp.logical_and(is_self, l == k)
+
+        @pl.when(jnp.logical_not(mine))
+        def _():
+            mom_remote(k).start()
+
+        @pl.when(mine)
+        def _():
+            mom_local(k).start()
 
     for k in (1, 3, 2):
         recv(b_id[k], recv_b.at[k - 1])

time: 64.9 us -> 63.9 us (0.985)
  Pallas kernels: 62.7 us -> 61.8 us
    pallas_call x1, Pallas kernels: 62.7 us -> 61.8 us  [per_device(): pl.pallas_call(kernel, out_shape=(pltpu.VMEM((TOK, KV), BF16), pltpu.VMEM...]
where the time goes in v7:
time: 63.9 us; the launch traced here: 63.8 us
  Pallas kernels  61.8 us (97%)
  local copies, waits for them, and re-layouts  1.42 us (2%)
  between operations  0.64 us (1%)
    pallas_call x1, Pallas kernels, per_device(): pl.pallas_call(kernel, out_shape=(pltpu.VMEM((TOK, KV), BF16), pltpu.VMEM...  61.8 us
    unnamed x2, local copies, waits for them, and re-layouts  1.42 us

profile of v7, /device:TPU:1, one launch (start us, length us, event | category | flops | bytes accessed | tf_op | source)
XLA Modules:
  0.0 63.8 jit_solution(16561852183977387339)
XLA Ops:
  0.6 61.8 %outer_sync.1 = (bf16[256,1024]{1,0:T(8,128)(2,1)S(1)}, f32[32,320]{1,0:T(8,128)S(1)}) custom-call(bf16[256,5120]{1,0:T(8,128)(2,1)} %tok_hbm.1, f32[1,5120]{1,0:T(1,128)} %bitcast.8, f32[1,1024]{1,0:T(1,128)} %bitcast.9, bf16[320,1024]{1,0:T(8,128)(2,1)} %base_hbm.1, bf16[320,1024]{1,0:T(8,128)(2,1)} %bitcast.6, f32[32,320]{1,0:T(8,128)} %bitcast.7), custom_call_target="tpu_custom_call" | custom-call | tf_op jit(solution)/shard_map/outer_sync/pallas_call | solution.py:466
  62.4 0.8 %copy.10 = bf16[256,1024]{1,0:T(8,128)(2,1)} copy(bf16[256,1024]{1,0:T(8,128)(2,1)S(1)} %get-tuple-element.6) | data formatting | bytes 1048576
  63.2 0.6 copy.11
